TPU v7x, 32 devices: a whole 2x2x4 slice. The times are simulated.
32 devices in a mesh: ctx: 8 (over y, x, core), tp: 4 (over z).
Axes of the slice: x: 2, y: 2, z: 4, core: 2. Of those that a mesh axis runs over, the one named last changes fastest.
Arguments:
- query_act: bfloat16 [4096, 4096], P('ctx', 'tp'), may hold values from -6 to 6
- key_act: bfloat16 [4096, 4096], P('ctx', 'tp'), may hold values from -6 to 6
- value_act: bfloat16 [4096, 4096], P('ctx', 'tp'), may hold values from -6 to 6
- out_grad: bfloat16 [4096, 4096], P('ctx', 'tp'), may hold values from -6 to 6
- filters: float32 [256, 4096], P('tp', 'ctx'), may hold values from -6 to 6
Outputs:
- query_grad: bfloat16 [4096, 4096], P('ctx', 'tp')
- key_grad: bfloat16 [4096, 4096], P('ctx', 'tp')
- value_grad: bfloat16 [4096, 4096], P('ctx', 'tp')
- filter_grad: float32 [256, 4096], P('tp', 'ctx')
All inputs are finite; a program needn't handle non-finite values.
Results may differ from a plain program's by a relative error of at most 0.006.
Values may be sent and summed in bfloat16 or wider, within the bound.
A program may use at most 128 MiB of HBM per device.

v0:
```python
import functools
import math

import jax
import jax.numpy as jnp
from jax import lax
from jax.experimental import pallas as pl
from jax.experimental.pallas import tpu as pltpu
from jax.sharding import PartitionSpec as P

GROUP_CH = 16


HIGH = lax.Precision.HIGHEST


def make_tables(outer_len, inner_len, full_len):
    half_rows = outer_len // 2
    freq_idx = lax.iota(jnp.int32, outer_len)[:, None]
    time_idx = lax.iota(jnp.int32, half_rows)[None, :]
    outer_angle = (freq_idx * time_idx % outer_len).astype(jnp.float32) * (
        2.0 * math.pi / outer_len
    )
    inner_idx = lax.iota(jnp.int32, inner_len)
    inner_angle = (inner_idx[:, None] * inner_idx[None, :] % inner_len).astype(jnp.float32) * (
        2.0 * math.pi / inner_len
    )
    inner_cos = jnp.cos(inner_angle)
    inner_sin = jnp.sin(inner_angle)
    forward_mat = jnp.concatenate(
        [jnp.concatenate([inner_cos, -inner_sin], 1), jnp.concatenate([inner_sin, inner_cos], 1)], 0
    )
    inverse_mat = jnp.concatenate(
        [jnp.concatenate([inner_cos, inner_sin], 1), jnp.concatenate([-inner_sin, inner_cos], 1)], 0
    )
    twist_angle = (freq_idx * inner_idx[None, :] % full_len).astype(jnp.float32) * (
        2.0 * math.pi / full_len
    )
    return (
        jnp.cos(outer_angle),
        jnp.sin(outer_angle),
        forward_mat,
        inverse_mat,
        jnp.cos(twist_angle),
        jnp.sin(twist_angle),
    )


def transform(signal, tables):
    outer_cos, outer_sin, forward_mat, inverse_mat, twist_cos, twist_sin = tables
    outer_len, half_rows = outer_cos.shape
    inner_len = twist_cos.shape[1]
    count = signal.shape[0]
    folded = signal.reshape(count, half_rows, inner_len)
    first_re = jnp.einsum("ka,cab->ckb", outer_cos, folded, precision=HIGH)
    first_im = -jnp.einsum("ka,cab->ckb", outer_sin, folded, precision=HIGH)
    turned_re = first_re * twist_cos + first_im * twist_sin
    turned_im = first_im * twist_cos - first_re * twist_sin
    joined = jnp.concatenate([turned_re, turned_im], -1).reshape(count * outer_len, 2 * inner_len)
    spectrum = jnp.dot(joined, forward_mat, precision=HIGH, preferred_element_type=jnp.float32)
    spectrum = spectrum.reshape(count, outer_len, 2 * inner_len)
    return (spectrum[..., :inner_len], spectrum[..., inner_len:])


def untransform(real_part, imag_part, tables):
    outer_cos, outer_sin, forward_mat, inverse_mat, twist_cos, twist_sin = tables
    outer_len, half_rows = outer_cos.shape
    inner_len = twist_cos.shape[1]
    count = real_part.shape[0]
    joined = jnp.concatenate([real_part, imag_part], -1).reshape(count * outer_len, 2 * inner_len)
    mixed = jnp.dot(joined, inverse_mat, precision=HIGH, preferred_element_type=jnp.float32)
    mixed = mixed.reshape(count, outer_len, 2 * inner_len)
    mixed_re = mixed[..., :inner_len]
    mixed_im = mixed[..., inner_len:]
    turned_re = mixed_re * twist_cos - mixed_im * twist_sin
    turned_im = mixed_re * twist_sin + mixed_im * twist_cos
    signal = jnp.einsum("ka,ckb->cab", outer_cos, turned_re, precision=HIGH) - jnp.einsum(
        "ka,ckb->cab", outer_sin, turned_im, precision=HIGH
    )
    return signal.reshape(count, half_rows * inner_len) / (2.0 * half_rows * inner_len)


def convolve(kv_prod, gated, spread, tables, filter_scale):
    channels = kv_prod.shape[0]
    groups_here = spread.shape[0]
    outer_len = tables[0].shape[0]
    inner_len = tables[4].shape[1]
    filt_re, filt_im = transform(spread, tables)
    filt_re = (filt_re * filter_scale)[:, None]
    filt_im = (filt_im * filter_scale)[:, None]
    both_re, both_im = transform(jnp.concatenate([kv_prod, gated], 0).astype(jnp.float32), tables)
    grouped = (groups_here, GROUP_CH, outer_len, inner_len)
    kv_re = both_re[:channels].reshape(grouped)
    kv_im = both_im[:channels].reshape(grouped)
    gated_re = both_re[channels:].reshape(grouped)
    gated_im = both_im[channels:].reshape(grouped)
    out_re = filt_re * kv_re - filt_im * kv_im
    out_im = filt_re * kv_im + filt_im * kv_re
    back_re = filt_re * gated_re + filt_im * gated_im
    back_im = filt_re * gated_im - filt_im * gated_re
    cross_re = jnp.sum(kv_re * gated_re + kv_im * gated_im, 1)
    cross_im = jnp.sum(kv_re * gated_im - kv_im * gated_re, 1)
    flat = (channels, outer_len, inner_len)
    stacked_re = jnp.concatenate([out_re.reshape(flat), back_re.reshape(flat), cross_re], 0)
    stacked_im = jnp.concatenate([out_im.reshape(flat), back_im.reshape(flat), cross_im], 0)
    signals = untransform(stacked_re, stacked_im, tables)
    conv_out = signals[:channels].astype(jnp.bfloat16)
    conv_grad = signals[channels : 2 * channels].astype(jnp.bfloat16)
    filt_grad = signals[2 * channels :] * filter_scale
    return (conv_out, conv_grad, filt_grad)


def product(first, second):
    return (first.astype(jnp.float32) * second.astype(jnp.float32)).astype(jnp.bfloat16)


def spectral_body(query_act, key_act, value_act, out_grad, filters):
    tokens = query_act.shape[0]
    ctx_size = lax.axis_size("ctx")
    seq_len = tokens * ctx_size
    full_len = 2 * seq_len
    inner_len = math.gcd(full_len, 1 << full_len.bit_length() // 2)
    outer_len = full_len // inner_len
    tables = make_tables(outer_len, inner_len, full_len)
    filter_scale = 1.0 / math.sqrt(seq_len)
    spread = lax.all_to_all(filters, "ctx", split_axis=0, concat_axis=1, tiled=True)
    kv_local = product(key_act, value_act).T
    gated_local = product(out_grad, query_act).T
    kv_prod, gated = (
        lax.all_to_all(kv_local, "ctx", split_axis=0, concat_axis=1, tiled=True),
        lax.all_to_all(gated_local, "ctx", split_axis=0, concat_axis=1, tiled=True),
    )
    conv_out, conv_grad, filt_grad = convolve(kv_prod, gated, spread, tables, filter_scale)
    filter_grad = lax.all_to_all(filt_grad, "ctx", split_axis=1, concat_axis=0, tiled=True)
    returned = (
        lax.all_to_all(conv_out, "ctx", split_axis=1, concat_axis=0, tiled=True),
        lax.all_to_all(conv_grad, "ctx", split_axis=1, concat_axis=0, tiled=True),
    )
    conv_local = returned[0].T
    grad_local = returned[1].T
    query_grad = product(out_grad, conv_local)
    key_grad = product(grad_local, value_act)
    value_grad = product(grad_local, key_act)
    return (query_grad, key_grad, value_grad, filter_grad)


LANES = 128
BLOCK = 2 * LANES
MAX_BLOCKS = 16
MESH = pl.DeviceIdType.MESH


def dot(left, right, contract):
    return lax.dot_general(left, right, (contract, ((), ())), preferred_element_type=jnp.float32)


def diagonal_sums(tile):
    rows = LANES
    while rows > 8:
        rows //= 2
        tile = tile[:rows] + pltpu.roll(tile[rows:], LANES - rows, 1)
    row = lax.broadcasted_iota(jnp.int32, tile.shape, 0)
    for step in (4, 2, 1):
        tile = jnp.where(row // step % 2 == 1, pltpu.roll(tile, LANES - step, 1), tile)
    return jnp.sum(tile, axis=0, keepdims=True)


def conv_kernel(
    n,
    scale,
    query_ref,
    key_ref,
    value_ref,
    grad_ref,
    filt_ref,
    ret_ref,
    fgrad_ref,
    outbox,
    inbox,
    results,
    taps,
    tap_grads,
    tap_rows,
    grad_rows,
    toeplitz,
    padded,
    conv_acc,
    back_acc,
    fwd_send,
    fwd_recv,
    ret_send,
    ret_recv,
    tap_send,
    tap_recv,
    fg_send,
    fg_recv,
    local_sems,
):
    me = lax.axis_index("ctx")
    tokens, chans = query_ref.shape
    parts = tokens // BLOCK
    rows_here = parts * GROUP_CH
    groups = inbox.shape[0]
    rows = inbox.shape[2]
    blocks = rows // GROUP_CH
    lanes_here = chans // n

    barrier = pltpu.get_barrier_semaphore()
    peers = [lax.rem(me + step, n) for step in range(1, n)]
    for peer in peers:
        pl.semaphore_signal(barrier, inc=1, device_id={"ctx": peer}, device_id_type=MESH)

    def fill(block, carry):
        lane = pl.ds(pl.multiple_of(block * LANES, LANES), LANES)
        first = block * (LANES // GROUP_CH)
        for part in range(parts):
            rows_of = pl.ds(part * BLOCK, BLOCK)
            for which, (one, two) in enumerate(((key_ref, value_ref), (grad_ref, query_ref))):
                prod = one[rows_of, lane].astype(jnp.float32) * two[rows_of, lane].astype(jnp.float32)
                turned = prod.astype(jnp.bfloat16).T
                outbox[pl.ds(first, LANES // GROUP_CH), which, pl.ds(part * GROUP_CH, GROUP_CH), :] = (
                    turned.reshape(LANES // GROUP_CH, GROUP_CH, BLOCK)
                )
        return carry

    lax.fori_loop(0, chans // LANES, fill, 0)

    def tap_copy(peer):
        return pltpu.make_async_remote_copy(
            src_ref=filt_ref.at[pl.ds(pl.multiple_of(peer * groups, groups), groups), :],
            dst_ref=taps.at[me],
            send_sem=tap_send.at[peer],
            recv_sem=tap_recv.at[me],
            device_id={"ctx": peer},
            device_id_type=MESH,
        )

    def fwd_copy(group, peer):
        return pltpu.make_async_remote_copy(
            src_ref=outbox.at[peer * groups + group],
            dst_ref=inbox.at[group, :, pl.ds(pl.multiple_of(me * rows_here, rows_here), rows_here), :],
            send_sem=fwd_send.at[group, peer],
            recv_sem=fwd_recv.at[group, me],
            device_id={"ctx": peer},
            device_id_type=MESH,
        )

    def fwd_arrival(group, peer):
        return pltpu.make_async_remote_copy(
            src_ref=outbox.at[peer * groups + group],
            dst_ref=inbox.at[group, :, pl.ds(pl.multiple_of(peer * rows_here, rows_here), rows_here), :],
            send_sem=fwd_send.at[group, peer],
            recv_sem=fwd_recv.at[group, peer],
            device_id={"ctx": peer},
            device_id_type=MESH,
        )

    def ret_copy(group, peer):
        return pltpu.make_async_remote_copy(
            src_ref=results.at[group, :, pl.ds(pl.multiple_of(peer * rows_here, rows_here), rows_here), :],
            dst_ref=ret_ref.at[me * groups + group],
            send_sem=ret_send.at[group, peer],
            recv_sem=ret_recv.at[group, me],
            device_id={"ctx": peer},
            device_id_type=MESH,
        )

    def ret_arrival(group, peer):
        return pltpu.make_async_remote_copy(
            src_ref=results.at[group, :, pl.ds(pl.multiple_of(peer * rows_here, rows_here), rows_here), :],
            dst_ref=ret_ref.at[peer * groups + group],
            send_sem=ret_send.at[group, peer],
            recv_sem=ret_recv.at[group, peer],
            device_id={"ctx": peer},
            device_id_type=MESH,
        )

    def fg_copy(peer):
        return pltpu.make_async_remote_copy(
            src_ref=tap_grads.at[peer],
            dst_ref=fgrad_ref.at[pl.ds(pl.multiple_of(me * groups, groups), groups), :],
            send_sem=fg_send.at[peer],
            recv_sem=fg_recv.at[me],
            device_id={"ctx": peer},
            device_id_type=MESH,
        )

    def fg_arrival(peer):
        return pltpu.make_async_remote_copy(
            src_ref=tap_grads.at[peer],
            dst_ref=fgrad_ref.at[pl.ds(pl.multiple_of(peer * groups, groups), groups), :],
            send_sem=fg_send.at[peer],
            recv_sem=fg_recv.at[peer],
            device_id={"ctx": peer},
            device_id_type=MESH,
        )

    def tap_arrival(peer):
        return pltpu.make_async_remote_copy(
            src_ref=filt_ref.at[pl.ds(pl.multiple_of(peer * groups, groups), groups), :],
            dst_ref=taps.at[peer],
            send_sem=tap_send.at[peer],
            recv_sem=tap_recv.at[peer],
            device_id={"ctx": peer},
            device_id_type=MESH,
        )

    pl.semaphore_wait(barrier, n - 1)
    for peer in peers:
        tap_copy(peer).start()

    def send_group(group, carry):
        for peer in peers:
            fwd_copy(group, peer).start()
        return carry

    lax.fori_loop(0, groups, send_group, 0)
    own_rows = pl.ds(pl.multiple_of(me * rows_here, rows_here), rows_here)
    own_groups = pl.ds(pl.multiple_of(me * groups, groups), groups)
    own_taps = pltpu.make_async_copy(filt_ref.at[own_groups, :], taps.at[me], local_sems.at[0])
    own_in = pltpu.make_async_copy(outbox.at[own_groups], inbox.at[:, :, own_rows, :], local_sems.at[1])
    own_taps.start()
    own_in.start()

    padded[pl.ds(rows, LANES), :] = jnp.zeros((LANES, BLOCK), jnp.bfloat16)
    toeplitz[pl.ds(LANES, LANES), pl.ds(0, LANES)] = jnp.zeros((LANES, LANES), jnp.bfloat16)
    own_taps.wait()
    own_in.wait()
    for peer in peers:
        tap_arrival(peer).wait_recv()

    tiles = rows * BLOCK // GROUP_CH // LANES
    per_dev = tiles // n
    for group in range(groups):
        for tile in range(tiles):
            tap_rows[group, pl.ds(tile, 1), :] = (
                taps[tile // per_dev, pl.ds(group, 1), pl.ds(tile % per_dev * LANES, LANES)] * scale
            )
    row_idx = lax.broadcasted_iota(jnp.int32, (LANES, LANES), 0)
    lane_idx = lax.broadcasted_iota(jnp.int32, (LANES, LANES), 1)
    upper = lane_idx >= row_idx

    def one_group(group, carry):
        before = jnp.zeros((LANES, LANES), jnp.float32)
        for tile in range(tiles):
            line = tap_rows[group, pl.ds(tile, 1), :]
            now = pltpu.roll(jnp.broadcast_to(line, (LANES, LANES)), 0, 1, stride=1, stride_axis=0)
            both = jnp.where(upper, now, before).astype(jnp.bfloat16)
            toeplitz[pl.ds(0, LANES), pl.ds(tile * LANES, LANES)] = both
            if tile + 1 < tiles:
                toeplitz[pl.ds(LANES, LANES), pl.ds((tile + 1) * LANES, LANES)] = both
            before = now
        for peer in peers:
            fwd_arrival(group, peer).wait_recv()
        padded[pl.ds(0, rows), :] = inbox[group, 1]
        turned = inbox[group, 0].T
        even_after = jnp.zeros((LANES, LANES), jnp.float32)
        carried = jnp.zeros((LANES, LANES), jnp.float32)
        conv_acc[...] = jnp.zeros(conv_acc.shape, jnp.float32)
        back_acc[...] = jnp.zeros(back_acc.shape, jnp.float32)
        for gap in reversed(range(blocks)):
            skip = gap * GROUP_CH
            count = rows - skip
            block_taps = toeplitz[:, pl.ds(gap * BLOCK, BLOCK)]
            conv_acc[pl.ds(skip, count), :] += dot(
                inbox[group, 0, pl.ds(0, count), :], block_taps, ((1,), (0,))
            )
            back_acc[pl.ds(0, count), :] += dot(
                padded[pl.ds(skip, count), :], block_taps, ((1,), (1,))
            )
            depth = -(-count // LANES) * LANES
            cross = dot(turned[:, :depth], padded[pl.ds(skip, depth), :], ((1,), (0,)))
            odd = cross[:LANES, LANES:] + carried
            even = cross[:LANES, :LANES] + cross[LANES:, LANES:]
            carried = cross[LANES:, :LANES]
            for tile, picked in (
                (2 * gap + 1, jnp.where(upper, odd, even_after)),
                (2 * gap, jnp.where(upper, even, odd)),
            ):
                grad_rows[group, pl.ds(tile, 1), :] = diagonal_sums(picked) * scale
            even_after = even
        results[group, 0] = conv_acc[...].astype(jnp.bfloat16)
        results[group, 1] = back_acc[...].astype(jnp.bfloat16)
        for peer in peers:
            ret_copy(group, peer).start()
        return carry

    lax.fori_loop(0, groups, one_group, 0)
    for group in range(groups):
        for tile in range(tiles):
            tap_grads[tile // per_dev, pl.ds(group, 1), pl.ds(tile % per_dev * LANES, LANES)] = (
                grad_rows[group, pl.ds(tile, 1), :]
            )
    for peer in peers:
        fg_copy(peer).start()
    own_ret = pltpu.make_async_copy(results.at[:, :, own_rows, :], ret_ref.at[own_groups], local_sems.at[2])
    own_fg = pltpu.make_async_copy(tap_grads.at[me], fgrad_ref.at[own_groups, :], local_sems.at[3])
    own_ret.start()
    own_fg.start()

    def finish_group(group, carry):
        for peer in peers:
            fwd_copy(group, peer).wait_send()
            ret_copy(group, peer).wait_send()
            ret_arrival(group, peer).wait_recv()
        return carry

    lax.fori_loop(0, groups, finish_group, 0)
    for peer in peers:
        tap_copy(peer).wait_send()
        fg_copy(peer).wait_send()
        fg_arrival(peer).wait_recv()
    own_ret.wait()
    own_fg.wait()


def finish_kernel(key_ref, value_ref, grad_ref, ret_ref, query_out, key_out, value_out):
    parts = key_ref.shape[0] // BLOCK
    for part in range(parts):
        rows_of = pl.ds(part * BLOCK, BLOCK)
        turned = []
        for which in range(2):
            piece = ret_ref[:, which, pl.ds(part * GROUP_CH, GROUP_CH), :]
            turned.append(piece.reshape(LANES, BLOCK).T.astype(jnp.float32))
        conv, back = turned
        query_out[rows_of, :] = (grad_ref[rows_of, :].astype(jnp.float32) * conv).astype(jnp.bfloat16)
        key_out[rows_of, :] = (back * value_ref[rows_of, :].astype(jnp.float32)).astype(jnp.bfloat16)
        value_out[rows_of, :] = (back * key_ref[rows_of, :].astype(jnp.float32)).astype(jnp.bfloat16)


def direct_body(query_act, key_act, value_act, out_grad, filters):
    tokens, chans = query_act.shape
    n = lax.axis_size("ctx")
    all_groups, taps_here = filters.shape
    groups = all_groups // n
    seq_len = tokens * n
    blocks = seq_len // BLOCK
    rows = blocks * GROUP_CH
    rows_here = rows // n
    vmem = pl.BlockSpec(memory_space=pltpu.VMEM)
    anywhere = pl.BlockSpec(memory_space=pl.ANY)
    dma = pltpu.SemaphoreType.DMA
    macs = groups * 3 * (rows + GROUP_CH) // 2 * blocks * BLOCK * BLOCK
    returned, fgrad = pl.pallas_call(
        functools.partial(conv_kernel, n, 1.0 / math.sqrt(seq_len)),
        out_shape=(
            jax.ShapeDtypeStruct((all_groups, 2, rows_here, BLOCK), jnp.bfloat16),
            jax.ShapeDtypeStruct((all_groups, taps_here), jnp.float32),
        ),
        in_specs=[vmem] * 5,
        out_specs=(anywhere, anywhere),
        scratch_shapes=[
            pltpu.VMEM((all_groups, 2, rows_here, BLOCK), jnp.bfloat16),
            pltpu.VMEM((groups, 2, rows, BLOCK), jnp.bfloat16),
            pltpu.VMEM((groups, 2, rows, BLOCK), jnp.bfloat16),
            pltpu.VMEM((n, groups, taps_here), jnp.float32),
            pltpu.VMEM((n, groups, taps_here), jnp.float32),
            pltpu.VMEM((groups, seq_len // LANES, LANES), jnp.float32),
            pltpu.VMEM((groups, seq_len // LANES, LANES), jnp.float32),
            pltpu.VMEM((BLOCK, seq_len), jnp.bfloat16),
            pltpu.VMEM((rows + LANES, BLOCK), jnp.bfloat16),
            pltpu.VMEM((rows, BLOCK), jnp.float32),
            pltpu.VMEM((rows, BLOCK), jnp.float32),
            dma((groups, n)),
            dma((groups, n)),
            dma((groups, n)),
            dma((groups, n)),
            dma((n,)),
            dma((n,)),
            dma((n,)),
            dma((n,)),
            dma((4,)),
        ],
        compiler_params=pltpu.CompilerParams(
            collective_id=0, has_side_effects=True, vmem_limit_bytes=48 * 1024 * 1024
        ),
        cost_estimate=pl.CostEstimate(flops=2 * macs, bytes_accessed=16 * tokens * chans, transcendentals=0),
    )(query_act, key_act, value_act, out_grad, filters)
    strip = pl.BlockSpec((tokens, LANES), lambda i: (0, i))
    side = jax.ShapeDtypeStruct((tokens, chans), jnp.bfloat16)
    query_grad, key_grad, value_grad = pl.pallas_call(
        finish_kernel,
        grid=(chans // LANES,),
        out_shape=(side, side, side),
        in_specs=[
            strip,
            strip,
            strip,
            pl.BlockSpec((LANES // GROUP_CH, 2, rows_here, BLOCK), lambda i: (i, 0, 0, 0)),
        ],
        out_specs=(strip, strip, strip),
        compiler_params=pltpu.CompilerParams(vmem_limit_bytes=32 * 1024 * 1024),
        cost_estimate=pl.CostEstimate(
            flops=3 * tokens * chans, bytes_accessed=16 * tokens * chans, transcendentals=0
        ),
    )(key_act, value_act, out_grad, returned)
    return (query_grad, key_grad, value_grad, fgrad)


def body(query_act, key_act, value_act, out_grad, filters):
    tokens, chans = query_act.shape
    n = lax.axis_size("ctx")
    groups = filters.shape[0] // n
    fits = (
        tokens % BLOCK == 0
        and chans % LANES == 0
        and filters.shape[1] % LANES == 0
        and groups % 8 == 0
        and tokens * n // BLOCK <= MAX_BLOCKS
    )
    if fits:
        return direct_body(query_act, key_act, value_act, out_grad, filters)
    return spectral_body(query_act, key_act, value_act, out_grad, filters)


def solution(mesh):
    return jax.shard_map(
        body,
        mesh=mesh,
        in_specs=(P("ctx", "tp"), P("ctx", "tp"), P("ctx", "tp"), P("ctx", "tp"), P("tp", "ctx")),
        out_specs=(P("ctx", "tp"), P("ctx", "tp"), P("ctx", "tp"), P("tp", "ctx")),
        check_vma=False,
    )
```

profile of v0, /device:TPU:0, one launch (start us, length us, event | category | flops | bytes accessed | tf_op | source)
XLA Modules:
  0.0 69.0 jit_solution(6167311909878822848)
XLA Ops:
  0.6 0.0 copy-start.1
  0.6 1.2 %copy-done.1 = bf16[512,1024]{1,0:T(8,128)(2,1)S(1)} copy-done((bf16[512,1024]{1,0:T(8,128)(2,1)S(1)}, bf16[512,1024]{1,0:T(8,128)(2,1)}, u32[]{:S(2)}) %copy-start.1) | copy-done | bytes 1048600
  1.9 0.0 copy-start.2
  1.9 1.2 %copy-done.2 = bf16[512,1024]{1,0:T(8,128)(2,1)S(1)} copy-done((bf16[512,1024]{1,0:T(8,128)(2,1)S(1)}, bf16[512,1024]{1,0:T(8,128)(2,1)}, u32[]{:S(2)}) %copy-start.2) | copy-done | bytes 1048600
  3.1 0.0 copy-start.3
  3.1 1.2 %copy-done.3 = bf16[512,1024]{1,0:T(8,128)(2,1)S(1)} copy-done((bf16[512,1024]{1,0:T(8,128)(2,1)S(1)}, bf16[512,1024]{1,0:T(8,128)(2,1)}, u32[]{:S(2)}) %copy-start.3) | copy-done | bytes 1048600
  4.3 0.0 copy-start.4
  4.3 1.2 %copy-done.4 = bf16[512,1024]{1,0:T(8,128)(2,1)S(1)} copy-done((bf16[512,1024]{1,0:T(8,128)(2,1)S(1)}, bf16[512,1024]{1,0:T(8,128)(2,1)}, u32[]{:S(2)}) %copy-start.4) | copy-done | bytes 1048600
  5.5 0.0 copy-start.5
  5.5 0.9 %copy-done.5 = f32[64,512]{1,0:T(8,128)S(1)} copy-done((f32[64,512]{1,0:T(8,128)S(1)}, f32[64,512]{1,0:T(8,128)}, u32[]{:S(2)}) %copy-start.5) | copy-done | bytes 131096
  6.4 56.0 %shard_map.84 = (bf16[64,2,32,256]{3,2,1,0:T(8,128)(2,1)}, f32[64,512]{1,0:T(8,128)S(1)}) custom-call(bf16[512,1024]{1,0:T(8,128)(2,1)S(1)} %copy-done.4, bf16[512,1024]{1,0:T(8,128)(2,1)S(1)} %copy-done.1, bf16[512,1024]{1,0:T(8,128)(2,1)S(1)} %copy-done.2, bf16[512,1024]{1,0:T(8,128)(2,1)S(1)} %copy-done.3, f32[64,512]{1,0:T(8,128)S(1)} %copy-done.5), custom_call_target="tpu_custom_call" | custom-call | flops 6845104128 | bytes 8388608 | tf_op jit(solution)/shard_map/pallas_call | solution.py:444
  62.4 0.0 copy-start
  62.4 1.6 %copy-done = bf16[64,2,32,256]{3,2,1,0:T(8,128)(2,1)S(1)} copy-done((bf16[64,2,32,256]{3,2,1,0:T(8,128)(2,1)S(1)}, bf16[64,2,32,256]{3,2,1,0:T(8,128)(2,1)}, u32[]{:S(2)}) %copy-start) | copy-done | bytes 2097176
  64.0 4.3 %shard_map.85 = (bf16[512,1024]{1,0:T(8,128)(2,1)}, bf16[512,1024]{1,0:T(8,128)(2,1)}, bf16[512,1024]{1,0:T(8,128)(2,1)}) custom-call(bf16[512,1024]{1,0:T(8,128)(2,1)S(1)} %copy-done.1, bf16[512,1024]{1,0:T(8,128)(2,1)S(1)} %copy-done.2, bf16[512,1024]{1,0:T(8,128)(2,1)S(1)} %copy-done.3, bf16[64,2,32,256]{3,2,1,0:T(8,128)(2,1)S(1)} %copy-done), custom_call_target="tpu_custom_call" | custom-call | flops 1572864 | bytes 8388608 | tf_op jit(solution)/shard_map/pallas_call | solution.py:481
  68.3 0.7 copy.10
Async XLA Ops:
  0.6 1.2 %copy-start.1 = (bf16[512,1024]{1,0:T(8,128)(2,1)S(1)}, bf16[512,1024]{1,0:T(8,128)(2,1)}, u32[]{:S(2)}) copy-start(bf16[512,1024]{1,0:T(8,128)(2,1)} %key_ref.3) | copy-start | bytes 3145732
  1.9 1.2 %copy-start.2 = (bf16[512,1024]{1,0:T(8,128)(2,1)S(1)}, bf16[512,1024]{1,0:T(8,128)(2,1)}, u32[]{:S(2)}) copy-start(bf16[512,1024]{1,0:T(8,128)(2,1)} %value_ref.3) | copy-start | bytes 3145732
  3.1 1.2 %copy-start.3 = (bf16[512,1024]{1,0:T(8,128)(2,1)S(1)}, bf16[512,1024]{1,0:T(8,128)(2,1)}, u32[]{:S(2)}) copy-start(bf16[512,1024]{1,0:T(8,128)(2,1)} %grad_ref.3) | copy-start | bytes 3145732
  4.3 1.2 %copy-start.4 = (bf16[512,1024]{1,0:T(8,128)(2,1)S(1)}, bf16[512,1024]{1,0:T(8,128)(2,1)}, u32[]{:S(2)}) copy-start(bf16[512,1024]{1,0:T(8,128)(2,1)} %query_ref.1) | copy-start | bytes 3145732
  5.5 0.9 %copy-start.5 = (f32[64,512]{1,0:T(8,128)S(1)}, f32[64,512]{1,0:T(8,128)}, u32[]{:S(2)}) copy-start(f32[64,512]{1,0:T(8,128)} %filt_ref.1) | copy-start | bytes 393220
  62.4 1.6 %copy-start = (bf16[64,2,32,256]{3,2,1,0:T(8,128)(2,1)S(1)}, bf16[64,2,32,256]{3,2,1,0:T(8,128)(2,1)}, u32[]{:S(2)}) copy-start(bf16[64,2,32,256]{3,2,1,0:T(8,128)(2,1)} %get-tuple-element.9.ret_ref) | copy-start | bytes 6291460
where the time goes:
time: 69.3 us; the launch traced here: 69 us
  Pallas kernels  60.3 us (87%)
  local copies, waits for them, and re-layouts  8.03 us (12%)
    pallas_call x1, Pallas kernels, direct_body(): pl.pallas_call(functools.partial(conv_kernel, n, 1.0 / math.sqrt(seq_len)...  56 us
    unnamed x13, local copies, waits for them, and re-layouts  8.03 us
    pallas_call x1, Pallas kernels, direct_body(): pl.pallas_call(finish_kernel, grid=(chans // LANES,), out_shape=(side, si...  4.28 us

commit v1 on v0

--- a/solution.py
+++ b/solution.py
@@ -147,6 +147,7 @@
 LANES = 128
 BLOCK = 2 * LANES
 MAX_BLOCKS = 16
+EARLY = 2
 MESH = pl.DeviceIdType.MESH
 
 
@@ -175,6 +176,7 @@
     filt_ref,
     ret_ref,
     fgrad_ref,
+    held,
     outbox,
     inbox,
     results,
@@ -195,6 +197,7 @@
     fg_send,
     fg_recv,
     local_sems,
+    load_sems,
 ):
     me = lax.axis_index("ctx")
     tokens, chans = query_ref.shape
@@ -210,20 +213,33 @@
     for peer in peers:
         pl.semaphore_signal(barrier, inc=1, device_id={"ctx": peer}, device_id_type=MESH)
 
-    def fill(block, carry):
-        lane = pl.ds(pl.multiple_of(block * LANES, LANES), LANES)
-        first = block * (LANES // GROUP_CH)
-        for part in range(parts):
-            rows_of = pl.ds(part * BLOCK, BLOCK)
-            for which, (one, two) in enumerate(((key_ref, value_ref), (grad_ref, query_ref))):
-                prod = one[rows_of, lane].astype(jnp.float32) * two[rows_of, lane].astype(jnp.float32)
-                turned = prod.astype(jnp.bfloat16).T
-                outbox[pl.ds(first, LANES // GROUP_CH), which, pl.ds(part * GROUP_CH, GROUP_CH), :] = (
-                    turned.reshape(LANES // GROUP_CH, GROUP_CH, BLOCK)
-                )
-        return carry
-
-    lax.fori_loop(0, chans // LANES, fill, 0)
+    arrays = (key_ref, value_ref, grad_ref, query_ref)
+
+    def load(which, dest):
+        strip = pl.ds(pl.multiple_of(dest * lanes_here, lanes_here), lanes_here)
+        return pltpu.make_async_copy(
+            arrays[which].at[:, strip], held.at[which, dest], load_sems.at[which, dest]
+        )
+
+    for step in range(1, n + 1):
+        for which in range(4):
+            load(which, lax.rem(me + step, n)).start()
+
+    def fill(dest):
+        for which in range(4):
+            load(which, dest).wait()
+        for strip in range(lanes_here // LANES):
+            lane = pl.ds(strip * LANES, LANES)
+            first = dest * groups + strip * (LANES // GROUP_CH)
+            for part in range(parts):
+                rows_of = pl.ds(part * BLOCK, BLOCK)
+                for which in range(2):
+                    one = held[2 * which, dest, rows_of, lane].astype(jnp.float32)
+                    two = held[2 * which + 1, dest, rows_of, lane].astype(jnp.float32)
+                    turned = (one * two).astype(jnp.bfloat16).T
+                    outbox[
+                        pl.ds(first, LANES // GROUP_CH), which, pl.ds(part * GROUP_CH, GROUP_CH), :
+                    ] = turned.reshape(LANES // GROUP_CH, GROUP_CH, BLOCK)
 
     def tap_copy(peer):
         return pltpu.make_async_remote_copy(
@@ -309,12 +325,22 @@
     for peer in peers:
         tap_copy(peer).start()
 
+    def fill_and_send(step, carry):
+        dest = lax.rem(me + step, n)
+        fill(dest)
+        for group in range(EARLY):
+            fwd_copy(group, dest).start()
+        return carry
+
+    lax.fori_loop(1, n, fill_and_send, 0)
+
     def send_group(group, carry):
         for peer in peers:
             fwd_copy(group, peer).start()
         return carry
 
-    lax.fori_loop(0, groups, send_group, 0)
+    lax.fori_loop(EARLY, groups, send_group, 0)
+    fill(me)
     own_rows = pl.ds(pl.multiple_of(me * rows_here, rows_here), rows_here)
     own_groups = pl.ds(pl.multiple_of(me * groups, groups), groups)
     own_taps = pltpu.make_async_copy(filt_ref.at[own_groups, :], taps.at[me], local_sems.at[0])
@@ -414,7 +440,10 @@
     own_fg.wait()
 
 
-def finish_kernel(key_ref, value_ref, grad_ref, ret_ref, query_out, key_out, value_out):
+def finish_kernel(
+    key_ref, value_ref, grad_ref, ret_ref, fgrad_ref, query_out, key_out, value_out, fgrad_out
+):
+    fgrad_out[...] = fgrad_ref[...]
     parts = key_ref.shape[0] // BLOCK
     for part in range(parts):
         rows_of = pl.ds(part * BLOCK, BLOCK)
@@ -437,7 +466,6 @@
     blocks = seq_len // BLOCK
     rows = blocks * GROUP_CH
     rows_here = rows // n
-    vmem = pl.BlockSpec(memory_space=pltpu.VMEM)
     anywhere = pl.BlockSpec(memory_space=pl.ANY)
     dma = pltpu.SemaphoreType.DMA
     macs = groups * 3 * (rows + GROUP_CH) // 2 * blocks * BLOCK * BLOCK
@@ -447,9 +475,10 @@
             jax.ShapeDtypeStruct((all_groups, 2, rows_here, BLOCK), jnp.bfloat16),
             jax.ShapeDtypeStruct((all_groups, taps_here), jnp.float32),
         ),
-        in_specs=[vmem] * 5,
+        in_specs=[anywhere] * 5,
         out_specs=(anywhere, anywhere),
         scratch_shapes=[
+            pltpu.VMEM((4, n, tokens, chans // n), jnp.bfloat16),
             pltpu.VMEM((all_groups, 2, rows_here, BLOCK), jnp.bfloat16),
             pltpu.VMEM((groups, 2, rows, BLOCK), jnp.bfloat16),
             pltpu.VMEM((groups, 2, rows, BLOCK), jnp.bfloat16),
@@ -470,31 +499,33 @@
             dma((n,)),
             dma((n,)),
             dma((4,)),
+            dma((4, n)),
         ],
         compiler_params=pltpu.CompilerParams(
-            collective_id=0, has_side_effects=True, vmem_limit_bytes=48 * 1024 * 1024
+            collective_id=0, has_side_effects=True, vmem_limit_bytes=56 * 1024 * 1024
         ),
         cost_estimate=pl.CostEstimate(flops=2 * macs, bytes_accessed=16 * tokens * chans, transcendentals=0),
     )(query_act, key_act, value_act, out_grad, filters)
     strip = pl.BlockSpec((tokens, LANES), lambda i: (0, i))
     side = jax.ShapeDtypeStruct((tokens, chans), jnp.bfloat16)
-    query_grad, key_grad, value_grad = pl.pallas_call(
+    fgrad_rows = pl.BlockSpec((LANES // GROUP_CH, taps_here), lambda i: (i, 0))
+    return pl.pallas_call(
         finish_kernel,
         grid=(chans // LANES,),
-        out_shape=(side, side, side),
+        out_shape=(side, side, side, jax.ShapeDtypeStruct(fgrad.shape, fgrad.dtype)),
         in_specs=[
             strip,
             strip,
             strip,
             pl.BlockSpec((LANES // GROUP_CH, 2, rows_here, BLOCK), lambda i: (i, 0, 0, 0)),
+            fgrad_rows,
         ],
-        out_specs=(strip, strip, strip),
-        compiler_params=pltpu.CompilerParams(vmem_limit_bytes=32 * 1024 * 1024),
+        out_specs=(strip, strip, strip, fgrad_rows),
+        compiler_params=pltpu.CompilerParams(vmem_limit_bytes=56 * 1024 * 1024),
         cost_estimate=pl.CostEstimate(
             flops=3 * tokens * chans, bytes_accessed=16 * tokens * chans, transcendentals=0
         ),
-    )(key_act, value_act, out_grad, returned)
-    return (query_grad, key_grad, value_grad, fgrad)
+    )(key_act, value_act, out_grad, returned, fgrad)
 
 
 def body(query_act, key_act, value_act, out_grad, filters):

time: 69.3 us -> 64.3 us (0.928)
  local copies, waits for them, and re-layouts: 8.03 us -> 0 us
  Pallas kernels: 60.3 us -> 63.4 us
    unnamed x13 -> x0, local copies, waits for them, and re-layouts: 8.03 us -> none
    pallas_call x1, Pallas kernels: 4.28 us -> 7.01 us  [direct_body(): pl.pallas_call(finish_kernel, grid=(chans // LANES,), out_shape=(side, si...]
where the time goes in v1:
time: 64.3 us; the launch traced here: 64 us
  Pallas kernels  63.4 us (99%)
    pallas_call x1, Pallas kernels, direct_body(): pl.pallas_call(functools.partial(conv_kernel, n, 1.0 / math.sqrt(seq_len)...  56.3 us
    pallas_call x1, Pallas kernels, direct_body(): pl.pallas_call(finish_kernel, grid=(chans // LANES,), out_shape=(side, si...  7.01 us

profile of v1, /device:TPU:0, one launch (start us, length us, event | category | flops | bytes accessed | tf_op | source)
XLA Modules:
  0.0 64.0 jit_solution(7043804907856115739)
XLA Ops:
  0.6 56.3 %shard_map.84 = (bf16[64,2,32,256]{3,2,1,0:T(8,128)(2,1)}, f32[64,512]{1,0:T(8,128)}) custom-call(bf16[512,1024]{1,0:T(8,128)(2,1)} %query_ref.1, bf16[512,1024]{1,0:T(8,128)(2,1)} %key_ref.3, bf16[512,1024]{1,0:T(8,128)(2,1)} %value_ref.3, bf16[512,1024]{1,0:T(8,128)(2,1)} %grad_ref.3, f32[64,512]{1,0:T(8,128)} %filt_ref.1), custom_call_target="tpu_custom_call" | custom-call | flops 6845104128 | bytes 8388608 | tf_op jit(solution)/shard_map/pallas_call | solution.py:472
  57.0 7.0 %shard_map.85 = (bf16[512,1024]{1,0:T(8,128)(2,1)}, bf16[512,1024]{1,0:T(8,128)(2,1)}, bf16[512,1024]{1,0:T(8,128)(2,1)}, f32[64,512]{1,0:T(8,128)}) custom-call(bf16[512,1024]{1,0:T(8,128)(2,1)} %key_ref.3, bf16[512,1024]{1,0:T(8,128)(2,1)} %value_ref.3, bf16[512,1024]{1,0:T(8,128)(2,1)} %grad_ref.3, bf16[64,2,32,256]{3,2,1,0:T(8,128)(2,1)} %get-tuple-element.6.ret_ref, ...), custom_call_target="tpu_custom_call" | custom-call | flops 1572864 | bytes 8388608 | tf_op jit(solution)/shard_map/pallas_call | solution.py:512

commit v2 on v1

--- a/solution.py
+++ b/solution.py
@@ -444,17 +444,17 @@
     key_ref, value_ref, grad_ref, ret_ref, fgrad_ref, query_out, key_out, value_out, fgrad_out
 ):
     fgrad_out[...] = fgrad_ref[...]
-    parts = key_ref.shape[0] // BLOCK
-    for part in range(parts):
-        rows_of = pl.ds(part * BLOCK, BLOCK)
+    per_strip = LANES // GROUP_CH
+    for strip in range(key_ref.shape[1] // LANES):
+        lane = pl.ds(strip * LANES, LANES)
         turned = []
         for which in range(2):
-            piece = ret_ref[:, which, pl.ds(part * GROUP_CH, GROUP_CH), :]
-            turned.append(piece.reshape(LANES, BLOCK).T.astype(jnp.float32))
+            piece = ret_ref[pl.ds(strip * per_strip, per_strip), which, :, :]
+            turned.append(piece.reshape(LANES, LANES).T.astype(jnp.float32))
         conv, back = turned
-        query_out[rows_of, :] = (grad_ref[rows_of, :].astype(jnp.float32) * conv).astype(jnp.bfloat16)
-        key_out[rows_of, :] = (back * value_ref[rows_of, :].astype(jnp.float32)).astype(jnp.bfloat16)
-        value_out[rows_of, :] = (back * key_ref[rows_of, :].astype(jnp.float32)).astype(jnp.bfloat16)
+        query_out[:, lane] = (grad_ref[:, lane].astype(jnp.float32) * conv).astype(jnp.bfloat16)
+        key_out[:, lane] = (back * value_ref[:, lane].astype(jnp.float32)).astype(jnp.bfloat16)
+        value_out[:, lane] = (back * key_ref[:, lane].astype(jnp.float32)).astype(jnp.bfloat16)
 
 
 def direct_body(query_act, key_act, value_act, out_grad, filters):
@@ -506,18 +506,20 @@
         ),
         cost_estimate=pl.CostEstimate(flops=2 * macs, bytes_accessed=16 * tokens * chans, transcendentals=0),
     )(query_act, key_act, value_act, out_grad, filters)
-    strip = pl.BlockSpec((tokens, LANES), lambda i: (0, i))
+    steps = tokens // LANES
+    halves = BLOCK // LANES
+    strip = pl.BlockSpec((LANES, chans), lambda i: (i, 0))
     side = jax.ShapeDtypeStruct((tokens, chans), jnp.bfloat16)
-    fgrad_rows = pl.BlockSpec((LANES // GROUP_CH, taps_here), lambda i: (i, 0))
+    fgrad_rows = pl.BlockSpec((all_groups // steps, taps_here), lambda i: (i, 0))
     return pl.pallas_call(
         finish_kernel,
-        grid=(chans // LANES,),
+        grid=(steps,),
         out_shape=(side, side, side, jax.ShapeDtypeStruct(fgrad.shape, fgrad.dtype)),
         in_specs=[
             strip,
             strip,
             strip,
-            pl.BlockSpec((LANES // GROUP_CH, 2, rows_here, BLOCK), lambda i: (i, 0, 0, 0)),
+            pl.BlockSpec((all_groups, 2, GROUP_CH, LANES), lambda i: (0, 0, i // halves, i % halves)),
             fgrad_rows,
         ],
         out_specs=(strip, strip, strip, fgrad_rows),
@@ -537,6 +539,7 @@
         and chans % LANES == 0
         and filters.shape[1] % LANES == 0
         and groups % 8 == 0
+        and filters.shape[0] % (tokens // LANES * 8) == 0
         and tokens * n // BLOCK <= MAX_BLOCKS
     )
     if fits:

time: 64.3 us -> 62.4 us (0.970)
  Pallas kernels: 63.4 us -> 61.5 us
    pallas_call x1, Pallas kernels: 7.01 us -> 5.18 us  [direct_body(): pl.pallas_call(finish_kernel, grid=(steps,), out_shape=(side, side, side,...]
where the time goes in v2:
time: 62.4 us; the launch traced here: 62.2 us
  Pallas kernels  61.5 us (99%)
  between operations  0.64 us (1%)
    pallas_call x1, Pallas kernels, direct_body(): pl.pallas_call(functools.partial(conv_kernel, n, 1.0 / math.sqrt(seq_len)...  56.3 us
    pallas_call x1, Pallas kernels, direct_body(): pl.pallas_call(finish_kernel, grid=(steps,), out_shape=(side, side, side,...  5.18 us

profile of v2, /device:TPU:0, one launch (start us, length us, event | category | flops | bytes accessed | tf_op | source)
XLA Modules:
  0.0 62.2 jit_solution(16871268548854670167)
XLA Ops:
  0.6 56.3 %shard_map.84 = (bf16[64,2,32,256]{3,2,1,0:T(8,128)(2,1)}, f32[64,512]{1,0:T(8,128)}) custom-call(bf16[512,1024]{1,0:T(8,128)(2,1)} %query_ref.1, bf16[512,1024]{1,0:T(8,128)(2,1)} %key_ref.3, bf16[512,1024]{1,0:T(8,128)(2,1)} %value_ref.3, bf16[512,1024]{1,0:T(8,128)(2,1)} %grad_ref.3, f32[64,512]{1,0:T(8,128)} %filt_ref.1), custom_call_target="tpu_custom_call" | custom-call | flops 6845104128 | bytes 8388608 | tf_op jit(solution)/shard_map/pallas_call | solution.py:472
  57.0 5.2 %shard_map.85 = (bf16[512,1024]{1,0:T(8,128)(2,1)}, bf16[512,1024]{1,0:T(8,128)(2,1)}, bf16[512,1024]{1,0:T(8,128)(2,1)}, f32[64,512]{1,0:T(8,128)}) custom-call(bf16[512,1024]{1,0:T(8,128)(2,1)} %key_ref.3, bf16[512,1024]{1,0:T(8,128)(2,1)} %value_ref.3, bf16[512,1024]{1,0:T(8,128)(2,1)} %grad_ref.3, bf16[64,2,32,256]{3,2,1,0:T(8,128)(2,1)} %get-tuple-element.6.ret_ref, ...), custom_call_target="tpu_custom_call" | custom-call | flops 1572864 | bytes 8388608 | tf_op jit(solution)/shard_map/pallas_call | solution.py:514
